TPU v7x, 256 devices: a whole 4x4x8 slice. The times are simulated.
256 devices in a mesh: section: 2 (over x_lo), tok: 64 (over y, z, core), head: 2 (over x_hi).
Axes of the slice: x: 4 (x_hi: 2, x_lo: 2; x = x_hi * 2 + x_lo), y: 4, z: 8, core: 2. Of those that a mesh axis runs over, the one named last changes fastest.
Arguments:
- queries: bfloat16 [2, 8192, 2048], P('section', 'tok', 'head'), may hold values from -6 to 6
- keyvals: bfloat16 [2, 8192, 2, 512], P('section', 'tok', None, 'head'), may hold values from -6 to 6
- span_req: int32 [2, 8192], P('section'), may hold values from 0 to 15, never falling along the last dimension, each value on 1 to 6144 neighbouring positions
- prefill_blocks: bfloat16 [3072, 2, 128, 512], P(('section', 'tok'), None, None, 'head'), may hold values from -6 to 6
- block_dest: int32 [3072], replicated, may hold values from 0 to 127, as said below
- out_weight: bfloat16 [2048, 2048], P('head'), may hold values from -0.125 to 0.125
Outputs:
- mixed: bfloat16 [2, 8192, 2048], P('section', 'tok', 'head')
- decode_blocks: bfloat16 [3072, 2, 128, 512], P(('section', 'tok'), None, None, 'head')
Inputs may be any that keep to these rules, and one draw needn't show every extreme that they name: `span_req`: along each half's 8192 positions the request number never falls; one request covers exactly 6144 positions and none covers more. `block_dest`: blocks of one half of section go to shards of the other half; no shard receives two blocks from one source shard, and every shard receives exactly 24 blocks.
All inputs are finite; a program needn't handle non-finite values.
Results may differ from a plain program's by a relative error of at most 0.009.
Values may be sent and summed in bfloat16 or wider, within the bound.
A program may use at most 128 MiB of HBM per device.

v0:
```python
import math

import jax
import jax.numpy as jnp
from jax import lax
from jax.sharding import PartitionSpec as P

HEADS = 32
KVH = 8
HD = 64


def swapped(value, axis, apart):
    mask = 2**apart
    pairs = [(source, source ^ mask) for source in range(lax.axis_size(axis))]
    return lax.ppermute(value, axis, pairs)


def pack_rows(blocks, dest_list, shard_count):
    targets = jnp.arange(shard_count, dtype=jnp.int32)
    matches = dest_list[None, :] == targets[:, None]
    present = jnp.any(matches, axis=1)
    picked = jnp.argmax(matches, axis=1)
    chosen = jnp.take(blocks, picked, axis=0)
    return jnp.where(present[:, None, None, None], chosen, jnp.zeros_like(chosen))


def compact_rows(received, sender_table, receiver, per_shard):
    present = jnp.any(sender_table == receiver, axis=1)
    ranking = jnp.cumsum(present.astype(jnp.int32)) - 1
    slot_ids = jnp.arange(per_shard, dtype=jnp.int32)
    matches = (ranking[None, :] == slot_ids[:, None]) & present[None, :]
    picked = jnp.argmax(matches, axis=1)
    return jnp.take(received, picked, axis=0)


def hand_over(prefill_blocks, block_dest):
    shard_count = lax.axis_size("tok")
    per_shard = prefill_blocks.shape[0]
    section_index = lax.axis_index("section")
    tok_index = lax.axis_index("tok")
    far_section = 1 - section_index
    dest_table = block_dest.reshape(-1, shard_count, per_shard)
    moved = swapped(prefill_blocks, "section", 0)
    sender_table = lax.dynamic_index_in_dim(dest_table, far_section, 0, keepdims=False)
    dest_list = lax.dynamic_index_in_dim(sender_table, tok_index, 0, keepdims=False)
    sending = pack_rows(moved, dest_list % shard_count, shard_count)
    received = lax.all_to_all(sending, "tok", split_axis=0, concat_axis=0, tiled=True)
    return compact_rows(received, sender_table, section_index * shard_count + tok_index, per_shard)


def per_device(queries, keyvals, span_req, prefill_blocks, block_dest, out_weight):
    tok_rows = queries.shape[1]
    local_kv = keyvals.shape[3] // HD
    group_size = HEADS // KVH
    first_query = lax.axis_index("tok") * tok_rows
    segments = span_req[0]
    grouped = queries[0].reshape(tok_rows, local_kv, group_size, HD)
    query_rows = first_query + jnp.arange(tok_rows, dtype=jnp.int32)
    query_segs = lax.dynamic_slice_in_dim(segments, first_query, tok_rows)
    score_scale = 1.0 / math.sqrt(HD)
    start_state = (
        jnp.full((tok_rows, local_kv, group_size), -1e30, jnp.float32),
        jnp.zeros((tok_rows, local_kv, group_size), jnp.float32),
        jnp.zeros((tok_rows, local_kv, group_size, HD), jnp.float32),
    )
    piece = lax.all_gather(keyvals[0], "tok", axis=0, tiled=True)
    key_rows = piece.shape[0]
    key_step = math.gcd(key_rows, 512)

    def one_turn(turn_idx, state):
        running, totals, accum_out = state
        offset = turn_idx * key_step
        key_block = lax.dynamic_slice_in_dim(piece, offset, key_step, 0)
        keys_part = key_block[:, 0].reshape(key_step, local_kv, HD)
        vals_part = key_block[:, 1].reshape(key_step, local_kv, HD)
        key_pos = offset + jnp.arange(key_step, dtype=jnp.int32)
        key_segs = lax.dynamic_slice_in_dim(segments, offset, key_step)
        allowed = (query_segs[:, None] == key_segs[None, :]) & (
            key_pos[None, :] <= query_rows[:, None]
        )
        scores = (
            jnp.einsum("qcgd,kcd->qcgk", grouped, keys_part, preferred_element_type=jnp.float32)
            * score_scale
        )
        scores = jnp.where(allowed[:, None, None, :], scores, -jnp.inf)
        newest = jnp.maximum(running, jnp.max(scores, axis=-1))
        expo = jnp.exp(scores - newest[..., None])
        factor = jnp.exp(running - newest)
        totals = totals * factor + jnp.sum(expo, axis=-1)
        weights = expo.astype(jnp.bfloat16)
        update = jnp.einsum(
            "qcgk,kcd->qcgd", weights, vals_part, preferred_element_type=jnp.float32
        )
        accum_out = accum_out * factor[..., None] + update
        return (newest, totals, accum_out)

    running, totals, accum_out = lax.fori_loop(0, key_rows // key_step, one_turn, start_state)
    attended = (
        (accum_out / totals[..., None])
        .reshape(tok_rows, local_kv * group_size * HD)
        .astype(jnp.bfloat16)
    )
    partial_out = jnp.dot(attended, out_weight, preferred_element_type=jnp.float32)
    mixed = lax.psum_scatter(
        partial_out.astype(jnp.bfloat16), "head", scatter_dimension=1, tiled=True
    )
    decode_blocks = hand_over(prefill_blocks, block_dest)
    return (mixed[None], decode_blocks)


def solution(mesh):
    return jax.shard_map(
        per_device,
        mesh=mesh,
        in_specs=(
            P("section", "tok", "head"),
            P("section", "tok", None, "head"),
            P("section", None),
            P(("section", "tok"), None, None, "head"),
            P(),
            P("head", None),
        ),
        out_specs=(P("section", "tok", "head"), P(("section", "tok"), None, None, "head")),
        check_vma=False,
    )
```

profile of v0, /device:TPU:1, one launch (start us, length us, event | category | flops | bytes accessed | tf_op | source)
XLA Modules:
  0.0 304.5 jit_solution(17722456661637793671)
XLA Ops:
  7.2 1.7 copy.17
  8.9 2.1 collective-permute-start
  12.2 1.1 copy.18
  14.8 63.1 %collective-permute-done = bf16[24,2,128,256]{3,2,1,0:T(8,128)(2,1)S(1)} collective-permute-done((bf16[24,2,128,256]{3,2,1,0:T(8,128)(2,1)}, bf16[24,2,128,256]{3,2,1,0:T(8,128)(2,1)S(1)}, u32[]{:S(2)}, u32[]{:S(2)}) %collective-permute-start) | collective-permute-done | bytes 3145760 | tf_op jit(solution)/shard_map/ppermute | solution.py:16
  77.8 5.5 %gather_fusion = bf16[64,2,128,256]{3,2,1,0:T(8,128)(2,1)} fusion(bf16[24,2,128,256]{3,2,1,0:T(8,128)(2,1)S(1)} %collective-permute-done, s32[1024]{0:T(1024)S(1)} %pad_clamp_fusion.1), kind=kCustom, calls=%fused_computation | custom fusion | bytes 16777472 | tf_op jit(solution)/shard_map/jit(_take)/gather | solution.py:24
  83.4 7.7 %select_select_fusion = bf16[64,2,128,256]{3,2,1,0:T(8,128)(2,1)} fusion(bf16[64,2,128,256]{3,2,1,0:T(8,128)(2,1)} %gather_fusion, pred[64]{0:T(512)(128)(4,1)S(1)} %compare_and_fusion.1, pred[64]{0:T(512)(128)(4,1)S(1)} %fusion.18), kind=kLoop, calls=%fused_computation.24 | loop fusion | flops 8388608 | bytes 16777344 | tf_op jit(solution)/shard_map/jit(_where)/select_n | solution.py:25
  91.0 14.7 %all-to-all-start = ((bf16[64,2,128,256]{3,2,1,0:T(8,128)(2,1)}), bf16[64,2,128,256]{3,2,1,0:T(8,128)(2,1)}, u32[]{:S(2)}, u32[]{:S(2)}) async-start(bf16[64,2,128,256]{3,2,1,0:T(8,128)(2,1)} %select_select_fusion), calls=%async_computation.1 | async-start | bytes 16777216 | tf_op jit(solution)/shard_map/all_to_all | solution.py:48
  105.8 78.6 %while.18 = (s32[]{:T(128)}, f32[128,4,4]{0,2,1:T(4,128)S(1)}, f32[128,4,4]{0,2,1:T(4,128)S(1)}, f32[128,4,4,64]{0,3,2,1:T(8,128)S(1)}, s32[128]{0:T(128)S(1)}, ...) while((s32[]{:T(128)}, f32[128,4,4]{0,2,1:T(4,128)S(1)}, ...), condition=%wide.region_3.4_spmd.clone, body=%wide.region_0.3_spmd.clone.sunk | while | flops 280570496 | bytes 15871719 | solution.py:98
  106.8 1.1 constant_dynamic-slice_fusion.5
  108.7 0.9 fusion.41
  109.6 1.1 fusion.43
  111.7 1.1 constant_dynamic-slice_fusion.5
  114.5 1.1 fusion.43
  116.6 1.1 constant_dynamic-slice_fusion.5
  118.5 0.9 fusion.41
  119.4 1.1 fusion.43
  121.5 1.1 constant_dynamic-slice_fusion.5
  123.4 0.9 fusion.41
  124.3 1.1 fusion.43
  126.5 1.1 constant_dynamic-slice_fusion.5
  129.2 1.1 fusion.43
  131.4 1.1 constant_dynamic-slice_fusion.5
  134.1 1.1 fusion.43
  136.3 1.1 constant_dynamic-slice_fusion.5
  138.2 0.9 fusion.41
  139.0 1.1 fusion.43
  141.2 1.1 constant_dynamic-slice_fusion.5
  144.0 1.1 fusion.43
  146.1 1.1 constant_dynamic-slice_fusion.5
  148.9 1.1 fusion.43
  151.0 1.1 constant_dynamic-slice_fusion.5
  153.8 1.1 fusion.43
  155.9 1.1 constant_dynamic-slice_fusion.5
  158.7 1.1 fusion.43
  160.9 1.1 constant_dynamic-slice_fusion.5
  163.6 1.1 fusion.43
  165.8 1.1 constant_dynamic-slice_fusion.5
  168.5 1.1 fusion.43
  170.7 1.1 constant_dynamic-slice_fusion.5
  173.4 1.1 fusion.43
  175.6 1.1 constant_dynamic-slice_fusion.5
  178.4 1.1 fusion.43
  180.5 1.1 constant_dynamic-slice_fusion.5
  183.3 1.1 fusion.43
  184.5 3.7 %convolution_convert_fusion = bf16[128,2048]{1,0:T(8,128)(2,1)} fusion(bf16[128,1024]{0,1:T(8,128)(2,1)S(1)} %bitcast.68, bf16[1024,2048]{1,0:T(8,128)(2,1)} %param.13), kind=kOutput, calls=%fused_computation.26 | convolution fusion | flops 537133056 | bytes 4980736 | tf_op jit(solution)/shard_map/dot_general | solution.py:104
  188.9 102.6 %all-to-all-done = bf16[64,2,128,256]{3,2,1,0:T(8,128)(2,1)} async-done(((bf16[64,2,128,256]{3,2,1,0:T(8,128)(2,1)}), bf16[64,2,128,256]{3,2,1,0:T(8,128)(2,1)}, u32[]{:S(2)}, u32[]{:S(2)}) %all-to-all-start) | async-done | bytes 8388640 | tf_op jit(solution)/shard_map/all_to_all | solution.py:48
  291.5 4.1 %gather_fusion.1 = bf16[24,2,128,256]{3,2,1,0:T(8,128)(2,1)S(1)} fusion(bf16[64,2,128,256]{3,2,1,0:T(8,128)(2,1)} %all-to-all-done, s32[1024]{0:T(1024)S(1)} %pad_clamp_fusion), kind=kCustom, calls=%fused_computation.1 | custom fusion | bytes 6291552 | tf_op jit(solution)/shard_map/jit(_take)/gather | solution.py:34
  295.6 2.0 broadcast_select_fusion
  (169 shorter events, 42.3 us)
Async XLA Ops:
  7.2 98.6 %all-gather.3.cloned.1.call-start = ((), (), s32[]{:S(2)}) async-start(), calls=%async_computation.3 | async-start | bytes 8519680 | tf_op jit(solution)/shard_map/all_gather | solution.py:67
  8.9 68.9 %collective-permute-start = (bf16[24,2,128,256]{3,2,1,0:T(8,128)(2,1)}, bf16[24,2,128,256]{3,2,1,0:T(8,128)(2,1)S(1)}, u32[]{:S(2)}, u32[]{:S(2)}) collective-permute-start(bf16[24,2,128,256]{3,2,1,0:T(8,128)(2,1)} %param.11), channel_id=1, source_target_pairs={{0,128},{128,0},{1,129},{129,1},{2,130},{130,2},{3,131},{131,3},{4... | collective-permute-start | bytes 9437192 | tf_op jit(solution)/shard_map/ppermute | solution.py:16
  91.0 14.7 %copy-start = (f32[128,4,4,64]{0,3,2,1:T(8,128)S(1)}, f32[128,4,4,64]{0,3,2,1:T(8,128)}, u32[]{:S(2)}) copy-start(f32[128,4,4,64]{0,3,2,1:T(8,128)} %custom-call.2) | copy-start | bytes 1572868
  91.0 200.4 %all-to-all-start = ((bf16[64,2,128,256]{3,2,1,0:T(8,128)(2,1)}), bf16[64,2,128,256]{3,2,1,0:T(8,128)(2,1)}, u32[]{:S(2)}, u32[]{:S(2)}) async-start(bf16[64,2,128,256]{3,2,1,0:T(8,128)(2,1)} %select_select_fusion), calls=%async_computation.1 | async-start | bytes 16777216 | tf_op jit(solution)/shard_map/all_to_all | solution.py:48
  105.7 191.9 %reduce-scatter.2.cloned.1.call-start = ((), (), s32[]{:S(2)}) async-start(), calls=%async_computation.2 | async-start | bytes 786432 | tf_op jit(solution)/shard_map/reduce_scatter | solution.py:105
Sparse Core Ops, SparseCore 0:
  11.1 89.6 all-gather.2
  188.3 22.1 reduce-scatter.1
where the time goes:
time: 306 us; the launch traced here: 304 us
  waiting for transfers between devices  166 us (54%)
  local copies, waits for them, and re-layouts  43.5 us (14%)
  matrix products  34.1 us (11%)
  other arithmetic  28.9 us (9%)
  starting transfers between devices  16.9 us (6%)
  between operations  14.1 us (5%)
    all_to_all x1, waiting for transfers between devices, hand_over(): lax.all_to_all(sending, 'tok', split_axis=0, concat_axis=0, tiled=True)  103 us
    ppermute x1, waiting for transfers between devices, swapped(): return lax.ppermute(value, axis, pairs)  63.1 us
    dot_general x16, matrix products, one_turn(): jnp.einsum('qcgk,kcd->qcgd', weights, vals_part, preferred_element_type=j...  17.9 us
    slice x16, local copies, waits for them, and re-layouts, one_turn(): vals_part = key_block[:, 1].reshape(key_step, local_kv, HD)  17.2 us
    all_to_all x1, starting transfers between devices, hand_over(): lax.all_to_all(sending, 'tok', split_axis=0, concat_axis=0, tiled=True)  14.7 us
    reduce_sum x16, other arithmetic, one_turn(): totals = totals * factor + jnp.sum(expo, axis=-1)  13.6 us
    dot_general x16, matrix products, one_turn(): jnp.einsum('qcgd,kcd->qcgk', grouped, keys_part, preferred_element_type=j...  12.5 us
    dynamic_slice x16, local copies, waits for them, and re-layouts, one_turn(): key_segs = lax.dynamic_slice_in_dim(segments, offset, key_step)  12.3 us
  transfers between devices with their start and end apart: 4, of which 2 were waited for; matrix products, arithmetic and copies ran while one was open for 34% of the time, Pallas kernels for 0%

commit v1 on v0

v1 whole, which is shorter than its diff:
```python
import functools
import math

import jax
import jax.numpy as jnp
from jax import lax
from jax.experimental import pallas as pl
from jax.experimental.pallas import tpu as pltpu
from jax.sharding import Mesh
from jax.sharding import PartitionSpec as P

HEADS = 32
KVH = 8
HD = 64
NY, NZ, NC = 4, 8, 2
BLK_DEV = 24
LONGEST = 6144
SHARDS = NY * NZ * NC
TOK = ("y", "z", "core")

Z_FIRST = (17, 13, 10, 4)
Y_SECOND = (18, 8)
Y_FIRST = (15, 7)
Z_SECOND = (20, 15, 11, 4)


def pack_rows(blocks, dest_list, shard_count):
    targets = jnp.arange(shard_count, dtype=jnp.int32)
    matches = dest_list[None, :] == targets[:, None]
    present = jnp.any(matches, axis=1)
    picked = jnp.argmax(matches, axis=1)
    chosen = jnp.take(blocks, picked, axis=0)
    return jnp.where(present[:, None, None, None], chosen, jnp.zeros_like(chosen))


def compact_rows(received, sender_table, receiver, per_shard):
    present = jnp.any(sender_table == receiver, axis=1)
    ranking = jnp.cumsum(present.astype(jnp.int32)) - 1
    slot_ids = jnp.arange(per_shard, dtype=jnp.int32)
    matches = (ranking[None, :] == slot_ids[:, None]) & present[None, :]
    picked = jnp.argmax(matches, axis=1)
    return jnp.take(received, picked, axis=0)


def hand_over_padded(prefill_blocks, block_dest):
    per_shard = prefill_blocks.shape[0]
    section = lax.axis_index("section")
    tok = (lax.axis_index("y") * NZ + lax.axis_index("z")) * NC + lax.axis_index("core")
    dest_table = block_dest.reshape(-1, SHARDS, per_shard)
    moved = lax.ppermute(prefill_blocks, "section", [(0, 1), (1, 0)])
    sender_table = lax.dynamic_index_in_dim(dest_table, 1 - section, 0, keepdims=False)
    dest_list = lax.dynamic_index_in_dim(sender_table, tok, 0, keepdims=False)
    sending = pack_rows(moved, dest_list % SHARDS, SHARDS)
    received = lax.all_to_all(sending, TOK, split_axis=0, concat_axis=0, tiled=True)
    return compact_rows(received, sender_table, section * SHARDS + tok, per_shard)


LANES = 32
POOL = 256
KEYS_COL, VALS_COL = 0, 8


def count_dot(a, b):
    return jnp.dot(a.astype(jnp.bfloat16), b.astype(jnp.bfloat16), preferred_element_type=jnp.float32)


def forward_share(number, ring, cap):
    half = ring // 2
    plus, minus, far = sum(number[1:half]), sum(number[half + 1 :]), number[half]
    even = jnp.floor((far + minus - plus + 1.0) * 0.5)
    return jnp.clip(even, jnp.maximum(0.0, far - cap), jnp.minimum(far, cap * 1.0))


def ring_lists(step, valid, before_of, total_of, ring, caps):
    half = ring // 2
    hot = [None] + [jnp.where(valid & (step == k), 1.0, 0.0) for k in range(1, ring)]
    tall = jnp.concatenate(hot[1:], axis=0)
    rows = step.shape[0]
    parts = lambda a: [None] + [a[k * rows : (k + 1) * rows] for k in range(ring - 1)]
    before, total = parts(count_dot(tall, before_of)), parts(count_dot(tall, total_of))
    number = [0.0] + total[1:]
    share = forward_share(number, ring, caps[-1])
    ahead_mask, back_mask = jnp.zeros_like(share), jnp.zeros_like(share)
    rank, spot = jnp.zeros_like(share), jnp.zeros_like(share)
    ahead_at = [sum(caps[:k]) for k in range(half)]
    back_at = [sum(caps) + at for at in ahead_at]
    far_ahead = hot[half] * jnp.where(before[half] < share, 1.0, 0.0)
    far_back = hot[half] - far_ahead
    for mask, place, at in (
        (far_ahead, before[half], ahead_at[half - 1]),
        (far_back, before[half] - share, back_at[half - 1]),
    ):
        rank += mask * place
        spot += mask * (place + at)
    ahead_mask += far_ahead
    back_mask += far_back
    for k in range(1, half):
        place = sum(number[k + 1 : half]) + share + before[k]
        rank += hot[k] * place
        spot += hot[k] * (place + ahead_at[k - 1])
        ahead_mask += hot[k]
        place = sum(number[half + 1 : ring - k]) + number[half] - share + before[ring - k]
        rank += hot[ring - k] * place
        spot += hot[ring - k] * (place + back_at[k - 1])
        back_mask += hot[ring - k]
    return ahead_mask, back_mask, rank, spot


def list_column(mask, rank, spot):
    slot = jnp.sum(mask * (rank + 1.0), axis=0, keepdims=True)
    code = jnp.sum(mask * spot, axis=0, keepdims=True)
    want = lax.broadcasted_iota(jnp.int32, (32, 1), 0).astype(jnp.float32) + 1.0
    return jnp.sum(jnp.where(slot == want, code, 0.0), axis=1, keepdims=True)


def wide_column(mask, rank, spot):
    want = lax.broadcasted_iota(jnp.int32, (32, 1), 0).astype(jnp.float32) + 1.0
    slot, code = mask * (rank + 1.0), mask * spot
    total = jnp.zeros((32, 1), jnp.float32)
    for row in range(mask.shape[0]):
        hit = slot[row : row + 1, :] == want
        total += jnp.sum(jnp.where(hit, code[row : row + 1, :], 0.0), axis=1, keepdims=True)
    return total


def route_plan(dest, other, y_first, me_y, me_z, core):
    rows, lanes = dest.shape
    ring_1, caps_1, ring_2, caps_2 = (NY, Y_FIRST, NZ, Z_SECOND) if y_first else (NZ, Z_FIRST, NY, Y_SECOND)
    me_1, me_2 = (me_y, me_z) if y_first else (me_z, me_y)
    lane = lax.broadcasted_iota(jnp.int32, (rows, lanes), 1)
    row = lax.broadcasted_iota(jnp.int32, (rows, lanes), 0)
    at_1, index = lane // LANES, (lane % LANES).astype(jnp.float32)
    valid = dest >= 0
    dest_y, dest_z = dest // (NZ * NC), dest // NC % NZ
    dest_1, dest_2 = (dest_y, dest_z) if y_first else (dest_z, dest_y)
    left = lax.broadcasted_iota(jnp.int32, (lanes, lanes), 0)
    right = lax.broadcasted_iota(jnp.int32, (lanes, lanes), 1)
    same = left // LANES == right // LANES
    one = lambda a: jnp.where(a, 1.0, 0.0)
    earlier = one(left < right)
    same_earlier, same_all = one(same & (left < right)), one(same)
    group_earlier = one(left // LANES < right // LANES)

    ahead, back, rank, spot = ring_lists(
        (dest_1 - at_1) & (ring_1 - 1), valid, same_earlier, same_all, ring_1, caps_1
    )
    own = one((row == me_2) & (at_1 == me_1))
    columns = [list_column(ahead * own, rank, index), list_column(back * own, rank, index)]
    moved = ahead + back
    spot_1 = jnp.where(moved > 0.5, POOL + spot, index)

    ahead, back, rank, spot = ring_lists(
        (dest_2 - row) & (ring_2 - 1), valid & (dest_1 == me_1), earlier, jnp.ones_like(earlier), ring_2, caps_2
    )
    own = one(row == me_2)
    columns += [list_column(ahead * own, rank, spot_1), list_column(back * own, rank, spot_1)]
    moved = ahead + back
    spot_2 = jnp.where(moved > 0.5, 2 * POOL + spot, spot_1)

    me = (me_y * NZ + me_z) * NC + core
    mine, theirs, far = one(dest == me), one(dest == me + 1 - 2 * core), one(other == me)

    def earlier_chips(hot):
        per_chip = count_dot(hot, same_all)
        if not y_first:
            below = jnp.zeros_like(hot)
            line = jnp.sum(hot, axis=1, keepdims=True)
            for r in range(rows):
                below += jnp.where(row > r, line[r : r + 1, :], 0.0)
            return below + count_dot(hot, group_earlier), per_chip
        below = jnp.zeros_like(hot)
        for r in range(rows):
            below += jnp.where(row > r, per_chip[r : r + 1, :], 0.0)
        whole = jnp.sum(hot, axis=0, keepdims=True)
        return below + count_dot(jnp.broadcast_to(whole, hot.shape), group_earlier), per_chip

    mine_at, mine_in = earlier_chips(mine)
    theirs_at, _ = earlier_chips(theirs)
    far_at, far_in = earlier_chips(far)
    second = core.astype(jnp.float32)
    columns.append(wide_column(theirs, theirs_at, spot_2))
    columns.append(
        wide_column(mine, mine_at + far_at + second * far_in, spot_2)
        + wide_column(far, mine_at + far_at + (1.0 - second) * mine_in, 3 * POOL + far_at)
    )
    return columns


def over_room(number, ring, caps):
    half = ring // 2
    share = forward_share(number, ring, caps[-1])
    worst = jnp.full_like(share, -1.0)
    for k in range(1, half + 1):
        ahead = sum(number[k:half]) + share
        back = sum(number[half + 1 : ring - k + 1]) + number[half] - share
        worst = jnp.maximum(worst, jnp.maximum(ahead, back) - caps[k - 1])
    return worst


def list_room(dest, y_first):
    rows, lanes = dest.shape
    ring_1, caps_1, ring_2, caps_2 = (NY, Y_FIRST, NZ, Z_SECOND) if y_first else (NZ, Z_FIRST, NY, Y_SECOND)
    lane = lax.broadcasted_iota(jnp.int32, (rows, lanes), 1)
    row = lax.broadcasted_iota(jnp.int32, (rows, lanes), 0)
    valid = dest >= 0
    dest_y, dest_z = dest // (NZ * NC), dest // NC % NZ
    dest_1, dest_2 = (dest_y, dest_z) if y_first else (dest_z, dest_y)
    step_1 = (dest_1 - lane // LANES) & (ring_1 - 1)
    step_2 = (dest_2 - row) & (ring_2 - 1)
    left = lax.broadcasted_iota(jnp.int32, (lanes, lanes), 0)
    right = lax.broadcasted_iota(jnp.int32, (lanes, lanes), 1)
    same = jnp.where(left // LANES == right // LANES, 1.0, 0.0)
    tall = jnp.concatenate([jnp.where(valid & (step_1 == k), 1.0, 0.0) for k in range(1, ring_1)], axis=0)
    tall = count_dot(tall, same)
    number = [0.0] + [tall[k * rows : (k + 1) * rows] for k in range(ring_1 - 1)]
    worst = jnp.max(over_room(number, ring_1, caps_1))
    for to in range(ring_1):
        here = valid & (dest_1 == to)
        number = [0.0] + [
            jnp.sum(jnp.where(here & (step_2 == k), 1.0, 0.0), axis=1, keepdims=True) for k in range(1, ring_2)
        ]
        worst = jnp.maximum(worst, jnp.max(over_room(number, ring_2, caps_2)))
    return worst


def plan_kernel(by_y, by_z, picks, room):
    section, core = lax.axis_index("section"), lax.axis_index("core")
    me_y, me_z = lax.axis_index("y"), lax.axis_index("z")
    keys = route_plan(by_y[section, core], by_y[section, 1 - core], False, me_y, me_z, core)
    vals = route_plan(by_z[1 - section, core], by_z[1 - section, 1 - core], True, me_y, me_z, core)
    lane = lax.broadcasted_iota(jnp.int32, (32, 128), 1)
    table = jnp.zeros((32, 128), jnp.float32)
    for base, columns in ((KEYS_COL, keys), (VALS_COL, vals)):
        for at, column in enumerate(columns):
            table = jnp.where(lane == base + at, column, table)
    picks[...] = table.astype(jnp.int32)
    worst = jnp.float32(-1.0)
    for half in range(2):
        for c in range(NC):
            worst = jnp.maximum(worst, list_room(by_y[half, c], False))
            worst = jnp.maximum(worst, list_room(by_z[half, c], True))
    room[...] = jnp.full(room.shape, worst, jnp.float32)


def plan_tables(block_dest):
    tables = (block_dest % SHARDS).reshape(2, NY, NZ, NC, BLK_DEV)
    tables = jnp.pad(tables, ((0, 0),) * 4 + ((0, LANES - BLK_DEV),), constant_values=-1)
    by_y = jnp.pad(
        tables.transpose(0, 3, 1, 2, 4).reshape(2, NC, NY, NZ * LANES),
        ((0, 0), (0, 0), (0, 8 - NY), (0, 0)), constant_values=-1,
    )
    by_z = tables.transpose(0, 3, 2, 1, 4).reshape(2, NC, NZ, NY * LANES)
    return by_y, by_z


def plan(block_dest):
    vmem = pl.BlockSpec(memory_space=pltpu.VMEM)
    return pl.pallas_call(
        plan_kernel,
        out_shape=(jax.ShapeDtypeStruct((32, 128), jnp.int32), jax.ShapeDtypeStruct((8, 128), jnp.float32)),
        in_specs=[vmem, vmem],
        out_specs=(vmem, vmem),
    )(*plan_tables(block_dest))


UNIT = 1024
SLAB = UNIT // NC
TOK_ROWS = 128
N_COPIES = 48


def pick(dst, count, picks, column, pools):
    def one(j, carry):
        code = picks[j, column]
        block = None
        for at, pool in enumerate(pools):
            if pool is None:
                continue
            row = jnp.clip(code - at * POOL, 0, pool.shape[0] - 1)
            found = pool[row]
            block = found if block is None else jnp.where(code >= at * POOL, found, block)
        dst[j] = block
        return carry

    lax.fori_loop(0, count, one, 0)


def move_kernel(
    picks, spread, kv_own, limits, weight, blocks, mixed, decoded,
    kv, w, keys_in, vals_in, vals_0, keys_st, keys_1, keys_2, keys_3, keys_end, vals_st, vals_1, vals_2, vals_3,
    high, total, accum, att, kept_out, away, got, local_sem, send_sem, recv_sem,
):
    section, core, head = lax.axis_index("section"), lax.axis_index("core"), lax.axis_index("head")
    y, z = lax.axis_index("y"), lax.axis_index("z")
    peers = {
        "x": {"section": 1 - section}, "core": {"core": 1 - core}, "head": {"head": 1 - head},
        "y+": {"y": (y + 1) % NY}, "y-": {"y": (y + NY - 1) % NY},
        "z+": {"z": (z + 1) % NZ}, "z-": {"z": (z + NZ - 1) % NZ},
    }
    count = [0]
    sends = []

    def send(src, dst, to):
        at = count[0]
        count[0] += 1
        copy = pltpu.make_async_remote_copy(
            src_ref=src, dst_ref=dst, send_sem=send_sem.at[at], recv_sem=recv_sem.at[at],
            device_id=peers[to], device_id_type=pl.DeviceIdType.MESH,
        )
        copy.start()
        sends.append(copy)
        return copy

    def sent(copies):
        for copy in copies:
            copy.wait_send()
            sends[:] = [c for c in sends if c is not copy]

    loads = [
        pltpu.make_async_copy(src, dst, local_sem.at[at])
        for at, (src, dst) in enumerate((
            (blocks.at[:, 1], vals_in), (kv_own, kv.at[(core * NY + y) * NZ + z]), (blocks.at[:, 0], keys_in), (weight, w),
        ))
    ]
    for load in loads:
        load.start()
    barrier = pltpu.get_barrier_semaphore()
    for peer in peers.values():
        pl.semaphore_signal(barrier, inc=1, device_id=peer, device_id_type=pl.DeviceIdType.MESH)
    pl.semaphore_wait(barrier, len(peers))

    def first_hops(stage, arrivals, axis, caps):
        cap, back = caps[0], sum(caps)
        return [
            send(stage.at[pl.ds(0, cap)], arrivals.at[pl.ds(0, cap)], axis + "+"),
            send(stage.at[pl.ds(cap, cap)], arrivals.at[pl.ds(back, cap)], axis + "-"),
        ]

    def next_hops(before, arrivals, axis, caps, k):
        came, at, back = sum(caps[: k - 1]), sum(caps[:k]), sum(caps)
        hops = []
        for copy, base, to in ((before[0], 0, "+"), (before[1], back, "-")):
            copy.wait_recv()
            hops.append(send(
                arrivals.at[pl.ds(base + came, caps[k])], arrivals.at[pl.ds(base + at, caps[k])], axis + to
            ))
        return hops

    def arrived(hops):
        for copy in hops:
            copy.wait_recv()

    def pick_lists(stage, caps, column, pools):
        pick(stage.at[pl.ds(0, caps[0])], caps[0], picks, column, pools)
        pick(stage.at[pl.ds(caps[0], caps[0])], caps[0], picks, column + 1, pools)

    def shard_at(c, yy, zz):
        return (c * NY + yy) * NZ + zz

    loads[1].wait()
    own = kv.at[shard_at(core, y, z)]
    kv_hops = [send(own, own, "z+"), send(own, own, "z-")]
    loads[0].wait()
    swap_vals = send(vals_in, vals_0, "x")
    loads[2].wait()
    pick_lists(keys_st, Z_FIRST, KEYS_COL, [keys_in])
    keys_from = keys_z = first_hops(keys_st, keys_1, "z", Z_FIRST)

    for k in range(1, NZ // 2):
        kv_hops[0].wait_recv()
        kv_hops[1].wait_recv()
        ahead = kv.at[shard_at(core, y, (z - k + NZ) % NZ)]
        back = kv.at[shard_at(core, y, (z + k) % NZ)]
        kv_hops[0] = send(ahead, ahead, "z+")
        if k < NZ // 2 - 1:
            kv_hops[1] = send(back, back, "z-")
    kv_hops[0].wait_recv()

    def line(yy):
        return kv.at[pl.ds(shard_at(core, yy, 0), NZ)]

    def part(yy, first):
        return kv.at[pl.ds(shard_at(core, yy, first), NZ // 2)]

    over, under = (y + 1) % NY, (y + NY - 1) % NY
    kv_y = [send(line(y), line(y), "y+"), send(line(y), line(y), "y-")]
    kv_core = [send(line(y), line(y), "core")]
    high[...] = jnp.full_like(high, -1e30)
    total[...] = jnp.zeros_like(total)
    accum[...] = jnp.zeros_like(accum)
    keys_z = next_hops(keys_z, keys_1, "z", Z_FIRST, 1)
    kv_y[0].wait_recv()
    kv_far = [send(part(under, 0), part(under, 0), "y+")]
    kv_core.append(send(line(under), line(under), "core"))
    kv_y[1].wait_recv()
    kv_far.append(send(part(over, NZ // 2), part(over, NZ // 2), "y-"))
    kv_core.append(send(line(over), line(over), "core"))
    swap_vals.wait_recv()
    pick_lists(vals_st, Y_FIRST, VALS_COL, [vals_0])
    vals_from = vals_y = first_hops(vals_st, vals_1, "y", Y_FIRST)
    keys_z = next_hops(keys_z, keys_1, "z", Z_FIRST, 2)
    arrived(kv_far)
    kv_core.append(send(line((y + 2) % NY), line((y + 2) % NY), "core"))
    arrived(kv_core)

    first_query = ((y * NZ + z) * NC + core) * TOK_ROWS
    local_kv, rows, _ = spread.shape

    def slab(half):
        unit, of_core = half // NC, half % NC
        at = shard_at(of_core, 0, 0) + unit * (SLAB // TOK_ROWS)
        block = kv[pl.ds(at, SLAB // TOK_ROWS)].reshape(SLAB, kv.shape[2])
        keys, vals = block[:, : local_kv * HD], block[:, local_kv * HD :].T
        row = lax.broadcasted_iota(jnp.int32, (SLAB, rows), 0)
        pos = unit * UNIT + of_core * TOK_ROWS + (row // TOK_ROWS) * (NC * TOK_ROWS) + row % TOK_ROWS
        keep = (pos >= limits[0:1, :]) & (pos <= limits[1:2, :])
        for c in range(local_kv):
            scores = lax.dot_general(
                keys, spread[c], (((1,), (1,)), ((), ())), preferred_element_type=jnp.float32
            )
            scores = jnp.where(keep, scores, -1e30)
            before = high[c : c + 1, :]
            now = jnp.maximum(before, jnp.max(scores, axis=0, keepdims=True))
            expo = jnp.exp(scores - now)
            factor = jnp.exp(before - now)
            high[c : c + 1, :] = now
            total[c : c + 1, :] = total[c : c + 1, :] * factor + jnp.sum(expo, axis=0, keepdims=True)
            accum[c] = accum[c] * factor + jnp.dot(
                vals[c * HD : (c + 1) * HD], expo.astype(jnp.bfloat16), preferred_element_type=jnp.float32
            )

    def units(low, top):
        def one(half, carry):
            start = half // NC * UNIT

            @pl.when((start < first_query + TOK_ROWS) & (start + UNIT > first_query - (LONGEST - 1)))
            def _():
                slab(half)

            return carry

        lax.fori_loop(low * NC, top * NC, one, 0)

    units(0, 2)
    keys_z = next_hops(keys_z, keys_1, "z", Z_FIRST, 3)
    vals_y = next_hops(vals_y, vals_1, "y", Y_FIRST, 1)
    arrived(keys_z)
    sent(keys_from)
    pick_lists(keys_st, Y_SECOND, KEYS_COL + 2, [keys_in, keys_1])
    keys_from = keys_y = first_hops(keys_st, keys_2, "y", Y_SECOND)
    arrived(vals_y)
    sent(vals_from)
    pick_lists(vals_st, Z_SECOND, VALS_COL + 2, [vals_0, vals_1])
    vals_from = vals_z = first_hops(vals_st, vals_2, "z", Z_SECOND)
    units(2, 6)
    keys_y = next_hops(keys_y, keys_2, "y", Y_SECOND, 1)
    vals_z = next_hops(vals_z, vals_2, "z", Z_SECOND, 1)
    arrived(keys_y)
    sent(keys_from)

    def between_cores(stage, arrivals, column, pools):
        pick(stage.at[pl.ds(0, BLK_DEV)], BLK_DEV, picks, column, pools)
        return send(stage.at[pl.ds(0, BLK_DEV)], arrivals, "core")

    keys_pools = [keys_in, keys_1, keys_2, keys_3]
    vals_pools = [vals_0, vals_1, vals_2, vals_3]
    crossing = between_cores(keys_st, keys_3, KEYS_COL + 4, keys_pools[:3])
    crossing.wait_recv()
    sent([crossing])
    pick(keys_st.at[pl.ds(0, BLK_DEV)], BLK_DEV, picks, KEYS_COL + 5, keys_pools)
    swap_keys = send(keys_st.at[pl.ds(0, BLK_DEV)], keys_end, "x")
    units(6, 8)
    vals_z = next_hops(vals_z, vals_2, "z", Z_SECOND, 2)

    group = rows // TOK_ROWS
    for c in range(local_kv):
        done = (accum[c] / total[c : c + 1, :]).astype(jnp.bfloat16)
        for g in range(group):
            at = (c * group + g) * HD
            att[at : at + HD, :] = done[:, g * TOK_ROWS : (g + 1) * TOK_ROWS]
    loads[3].wait()
    width = w.shape[1] // 2
    attended = att[...].T

    def columns(first):
        return jnp.dot(attended, w[:, pl.ds(pl.multiple_of(first, width), width)], preferred_element_type=jnp.float32)

    away[...] = columns((1 - head) * width).astype(jnp.bfloat16)
    over_heads = send(away, got, "head")
    kept_out[...] = columns(head * width)
    vals_z = next_hops(vals_z, vals_2, "z", Z_SECOND, 3)
    over_heads.wait_recv()
    mixed[...] = (kept_out[...] + got[...].astype(jnp.float32)).astype(jnp.bfloat16)

    arrived(vals_z)
    sent(vals_from)
    crossing = between_cores(vals_st, vals_3, VALS_COL + 4, vals_pools[:3])
    crossing.wait_recv()
    sent([crossing])
    sent([swap_vals])
    pick(vals_in, BLK_DEV, picks, VALS_COL + 5, vals_pools)
    vals_out = pltpu.make_async_copy(vals_in, decoded.at[:, 1], local_sem.at[4])
    vals_out.start()
    swap_keys.wait_recv()
    keys_out = pltpu.make_async_copy(keys_end, decoded.at[:, 0], local_sem.at[5])
    keys_out.start()
    vals_out.wait()
    keys_out.wait()
    sent(sends[:])


def move_and_multiply(picks, spread, kv_own, limits, weight, blocks):
    local_kv, rows, _ = spread.shape
    half = lambda n: pltpu.VMEM((n,) + blocks.shape[2:], blocks.dtype)
    vmem, hbm = pl.BlockSpec(memory_space=pltpu.VMEM), pl.BlockSpec(memory_space=pl.ANY)
    width = weight.shape[1] // 2
    return pl.pallas_call(
        move_kernel,
        out_shape=(
            jax.ShapeDtypeStruct((TOK_ROWS, width), jnp.bfloat16),
            jax.ShapeDtypeStruct(blocks.shape, blocks.dtype),
        ),
        in_specs=[pl.BlockSpec(memory_space=pltpu.SMEM), vmem, hbm, vmem, hbm, hbm],
        out_specs=(vmem, hbm),
        scratch_shapes=[
            pltpu.VMEM((SHARDS,) + kv_own.shape, jnp.bfloat16),
            pltpu.VMEM(weight.shape, jnp.bfloat16),
            half(BLK_DEV), half(BLK_DEV), half(BLK_DEV),
            half(2 * max(Z_FIRST[0], Y_SECOND[0])), half(2 * sum(Z_FIRST)), half(2 * sum(Y_SECOND)), half(BLK_DEV), half(BLK_DEV),
            half(2 * max(Y_FIRST[0], Z_SECOND[0])), half(2 * sum(Y_FIRST)), half(2 * sum(Z_SECOND)), half(BLK_DEV),
            pltpu.VMEM((8, rows), jnp.float32),
            pltpu.VMEM((8, rows), jnp.float32),
            pltpu.VMEM((local_kv, HD, rows), jnp.float32),
            pltpu.VMEM((weight.shape[0], TOK_ROWS), jnp.bfloat16),
            pltpu.VMEM((TOK_ROWS, width), jnp.float32),
            pltpu.VMEM((TOK_ROWS, width), jnp.bfloat16),
            pltpu.VMEM((TOK_ROWS, width), jnp.bfloat16),
            pltpu.SemaphoreType.DMA((6,)),
            pltpu.SemaphoreType.DMA((N_COPIES,)),
            pltpu.SemaphoreType.DMA((N_COPIES,)),
        ],
        compiler_params=pltpu.CompilerParams(
            collective_id=0, has_side_effects=True, vmem_limit_bytes=63 * 1024 * 1024
        ),
        cost_estimate=pl.CostEstimate(flops=10**10, bytes_accessed=20 * 2**20, transcendentals=10**7),
    )(picks, spread, kv_own, limits, weight, blocks)


def per_device(queries, keyvals, span_req, prefill_blocks, block_dest, out_weight):
    tok_rows = queries.shape[1]
    local_kv = keyvals.shape[3] // HD
    group = HEADS // KVH
    tok = (lax.axis_index("y") * NZ + lax.axis_index("z")) * NC + lax.axis_index("core")
    first_query = tok * tok_rows
    segments = span_req[0]

    picks, room = plan(block_dest)
    own_segments = lax.dynamic_slice_in_dim(segments, first_query, tok_rows)
    starts = jnp.sum(segments[None, :] < own_segments[:, None], axis=1).astype(jnp.int32)
    places = first_query + jnp.arange(tok_rows, dtype=jnp.int32)
    limits = jnp.stack([jnp.tile(starts, group), jnp.tile(places, group)])
    scaled = queries[0].reshape(tok_rows, local_kv, group, HD) * jnp.bfloat16(1.0 / math.sqrt(HD))
    own = jnp.eye(local_kv, dtype=jnp.bfloat16)
    spread = jnp.einsum("qcgd,ce->cgqed", scaled, own).reshape(local_kv, group * tok_rows, local_kv * HD)
    kv_own = keyvals[0].reshape(tok_rows, 2 * local_kv * HD)
    mixed, routed = move_and_multiply(picks, spread, kv_own, limits, out_weight, prefill_blocks)
    decode_blocks = lax.cond(
        room[0, 0] <= 0.0,
        lambda done, blocks, dest: done,
        lambda done, blocks, dest: hand_over_padded(blocks, dest),
        routed, prefill_blocks, block_dest,
    )
    return mixed[None], decode_blocks


def solution(mesh):
    fine = Mesh(mesh.devices.reshape(2, NY, NZ, NC, 2), ("section",) + TOK + ("head",))
    return jax.shard_map(
        per_device,
        mesh=fine,
        in_specs=(
            P("section", TOK, "head"),
            P("section", TOK, None, "head"),
            P("section", None),
            P(("section",) + TOK, None, None, "head"),
            P(),
            P("head", None),
        ),
        out_specs=(P("section", TOK, "head"), P(("section",) + TOK, None, None, "head")),
        check_vma=False,
    )
```

time: 306 us -> 228 us (0.75)
  Pallas kernels: 0 us -> 210 us
  waiting for transfers between devices: 166 us -> 0 us
  matrix products: 34.1 us -> 0 us
  local copies, waits for them, and re-layouts: 43.5 us -> 13.4 us
  other arithmetic: 28.9 us -> 3.14 us
  starting transfers between devices: 16.9 us -> 0 us
  between operations: 14.1 us -> 1.42 us
    pallas_call x0 -> x2, Pallas kernels: none -> 210 us  [the longest x1 207 us: move_and_multiply(): pl.pallas_call(move_kernel, out_shape=(jax.ShapeDtypeStruct((TOK_ROWS, wi...]
    all_to_all x1 -> x0, waiting for transfers between devices: 103 us -> none  [hand_over(): lax.all_to_all(sending, 'tok', split_axis=0, concat_axis=0, tiled=True)]
    ppermute x1 -> x0, waiting for transfers between devices: 63.1 us -> none  [swapped(): return lax.ppermute(value, axis, pairs)]
    dot_general x33 -> x0, matrix products: 34.1 us -> none  [the longest x16 17.9 us: one_turn(): jnp.einsum('qcgk,kcd->qcgd', weights, vals_part, preferred_element_type=j...]
    slice x16 -> x1, local copies, waits for them, and re-layouts: 17.2 us -> 1.18 us  [per_device(): room[0, 0] <= 0.0]
    all_to_all x1 -> x0, starting transfers between devices: 14.7 us -> none  [hand_over(): lax.all_to_all(sending, 'tok', split_axis=0, concat_axis=0, tiled=True)]
    dynamic_slice x17 -> x0, local copies, waits for them, and re-layouts: 12.9 us -> none  [the longest x16 12.3 us: one_turn(): key_segs = lax.dynamic_slice_in_dim(segments, offset, key_step)]
    reduce_sum x16 -> x1, other arithmetic: 13.6 us -> 1.34 us  [per_device(): jnp.sum(segments[None, :] < own_segments[:, None], axis=1).astype(jnp.int32)]
  transfers between devices with their start and end apart: 4 -> 0, of which waited for: 2 -> 0; matrix products, arithmetic and copies ran while one was open for 34% -> 0% of each run, Pallas kernels for 0% -> 0%
where the time goes in v1:
time: 228 us
  Pallas kernels  210 us (92%)
  local copies, waits for them, and re-layouts  13.4 us (6%)
  other arithmetic  3.14 us (1%)
    pallas_call x1, Pallas kernels, move_and_multiply(): pl.pallas_call(move_kernel, out_shape=(jax.ShapeDtypeStruct((TOK_ROWS, wi...  207 us
    unnamed x8, local copies, waits for them, and re-layouts  8 us

profile of v1, /device:TPU:1, one launch (start us, length us, event | category | flops | bytes accessed | tf_op | source)
XLA Modules:
  0.0 227.8 jit_solution(14519744458781669455)
XLA Ops:
  0.6 0.7 dynamic-slice_bitcast_fusion
  1.3 1.3 convert_reduce_fusion
  2.7 0.6 pad_add_fusion.limits
  3.3 0.7 add_select_fusion
  4.0 0.1 reshape.102
  4.2 0.7 reshape.104.by_z
  4.9 0.1 reshape.103
  5.0 0.6 pad.9.by_y
  5.7 2.3 %shard_map.77 = (s32[32,128]{1,0:T(8,128)}, f32[8,128]{1,0:T(8,128)}) custom-call(s32[2,2,8,256]{3,2,1,0:T(8,128)} %pad.9.by_y, s32[2,2,8,128]{3,2,1,0:T(8,128)} %reshape.104.by_z), custom_call_target="tpu_custom_call" | custom-call | tf_op jit(solution)/shard_map/pallas_call | solution.py:258
  8.0 1.2 slice.3
  9.8 1.6 copy.23
  11.4 1.1 copy.20
  12.5 0.2 copy.21
  12.8 0.5 multiply_bitcast_fusion
  13.2 0.4 reshape.105
  13.7 1.3 copy.22.spread
  15.0 0.0 copy-start.1
  15.0 207.3 %shard_map.78 = (bf16[128,1024]{1,0:T(8,128)(2,1)}, bf16[24,2,128,256]{3,2,1,0:T(8,128)(2,1)}) custom-call(s32[32,128]{1,0:T(8,128)} %get-tuple-element.18.picks, bf16[4,512,256]{2,1,0:T(8,128)(2,1)} %copy.22.spread, bf16[128,512]{1,0:T(8,128)(2,1)} %bitcast.30, s32[2,512]{1,0:T(2,128)} %pad_add_fusion.limits, bf16[1024,2048]{1,0:T(8,128)(2,1)} %weight.1, ...), custom_call_target="tpu_custom_call" | custom-call | flops 10000000000 | bytes 20971520 | tf_op jit(solution)/shard_map/pallas_call | solution.py:517
  222.3 0.0 copy-done.1
  222.3 0.0 copy-start
  222.3 0.2 conditional.1
  222.5 0.7 copy-done
  223.2 0.7 copy.28
  223.9 3.9 %copy.29 = bf16[24,2,128,256]{3,2,1,0:T(8,128)(2,1)} copy(bf16[24,2,128,256]{3,2,1,0:T(8,128)(2,1)} %get-tuple-element.28) | data formatting | bytes 6291456
  (8 shorter events, 0.1 us)
Async XLA Ops:
  15.0 207.3 %copy-start.1 = (s32[3072]{0:T(1024)S(1)}, s32[3072]{0:T(1024)}, u32[]{:S(2)}) copy-start(s32[3072]{0:T(1024)} %param.12) | copy-start | bytes 36868
  222.3 1.0 copy-start

commit v2 on v1

--- a/solution.py
+++ b/solution.py
@@ -266,30 +266,121 @@
 UNIT = 1024
 SLAB = UNIT // NC
 TOK_ROWS = 128
-N_COPIES = 48
-
-
-def pick(dst, count, picks, column, pools):
+PARTS = 2
+REQUESTS = 16
+
+
+RATE = {"x": 0.0475, "y": 0.0475, "z": 0.0475, "core": 0.24, "head": 0.0475}
+LATENCY = 1.8
+DEPTH = {"x": 1, "y": 1, "z": 2, "core": 4, "head": 1}
+FIRST_Z = {"tokens": 0, "keys0": 1, "vals0": 2, "keys1": 3, "vals1": 4}
+FIRST_Y = {"tokens": 0, "vals0": 1, "far": 1.5, "keys0": 2, "vals1": 3, "keys1": 4}
+UNIT_US = 5.7
+SLACK = 3.0
+
+
+class Transfer:
+    def __init__(self, link, megabytes, *moves, small=False):
+        self.link, self.megabytes, self.moves, self.small = link, megabytes, moves, small
+        self.copies, self.ends, self.left = None, None, megabytes
+
+
+class Order:
+    def __init__(self, send):
+        self.send, self.now = send, 0.0
+        self.queues = {link: [] for link in RATE}
+        self.busy = {link: [] for link in RATE}
+        self.seen = dict.fromkeys(RATE, 0.0)
+
+    def advance(self, link):
+        while self.busy[link]:
+            span = min(t.left for t in self.busy[link]) * len(self.busy[link]) / RATE[link]
+            ended = self.seen[link] + span <= self.now
+            span = min(span, self.now - self.seen[link])
+            part = span * RATE[link] / len(self.busy[link])
+            for t in self.busy[link]:
+                t.left -= part
+            self.seen[link] += span
+            if not ended:
+                break
+            self.busy[link] = [t for t in self.busy[link] if t.left > 1e-9]
+        self.seen[link] = self.now
+
+    def foresee(self, link):
+        at, gone = self.now, 0.0
+        todo = sorted(self.busy[link], key=lambda t: t.left)
+        for rank, t in enumerate(todo):
+            at += (t.left - gone) * (len(todo) - rank) / RATE[link]
+            gone = t.left
+            t.ends = at
+
+    def post(self, transfer, rank):
+        self.queues[transfer.link].append((rank, transfer))
+        self.issue()
+
+    def issue(self):
+        for link, queue in self.queues.items():
+            self.advance(link)
+            while queue and (len(self.busy[link]) < DEPTH[link] or min(queue, key=lambda e: e[0])[1].small):
+                entry = min(queue, key=lambda e: e[0])
+                queue.remove(entry)
+                self.busy[link].append(entry[1])
+                entry[1].copies = [self.send(*move) for move in entry[1].moves]
+            self.foresee(link)
+
+    def run(self, chains):
+        waiting = []
+
+        def step(name, chain):
+            for wanted in chain:
+                if wanted is None:
+                    waiting.append((name, None, chain))
+                    return
+                if wanted.copies is None and all(wanted is not t for q in self.queues.values() for _, t in q):
+                    rank = (FIRST_Y if wanted.link == "y" else FIRST_Z).get(name, 9)
+                    self.post(wanted, rank)
+                waiting.append((name, wanted, chain))
+                return
+
+        for name, chain in chains:
+            step(name, chain)
+        while waiting:
+            self.issue()
+            ready = [w for w in waiting if w[1] is not None and w[1].ends is not None]
+            compute = [w for w in waiting if w[1] is None]
+            first = min(ready, key=lambda w: w[1].ends) if ready else None
+            if compute and (first is None or first[1].ends + LATENCY - self.now > SLACK):
+                entry = compute[0]
+                self.now += UNIT_US
+            elif first is not None:
+                entry = first
+                self.now = max(self.now, first[1].ends + LATENCY)
+                for copy in first[1].copies:
+                    copy.wait_recv()
+            else:
+                self.now = min(t.ends for busy in self.busy.values() for t in busy) + 1e-6
+                continue
+            waiting = [w for w in waiting if w is not entry]
+            step(entry[0], entry[2])
+
+
+def pick(dst, first, count, picks, column, pools):
     def one(j, carry):
         code = picks[j, column]
         block = None
         for at, pool in enumerate(pools):
-            if pool is None:
-                continue
             row = jnp.clip(code - at * POOL, 0, pool.shape[0] - 1)
             found = pool[row]
             block = found if block is None else jnp.where(code >= at * POOL, found, block)
-        dst[j] = block
+        dst[first + j] = block
         return carry
 
     lax.fori_loop(0, count, one, 0)
 
 
-def move_kernel(
-    picks, spread, kv_own, limits, weight, blocks, mixed, decoded,
-    kv, w, keys_in, vals_in, vals_0, keys_st, keys_1, keys_2, keys_3, keys_end, vals_st, vals_1, vals_2, vals_3,
-    high, total, accum, att, kept_out, away, got, local_sem, send_sem, recv_sem,
-):
+def move_kernel(picks, queries, kv_own, requests, weight, blocks, mixed, decoded, *scratch):
+    kv, w, spread, high, total, accum, att, kept_out, away, got, local_sem, send_sem, recv_sem = scratch[:13]
+    buffers = scratch[13:]
     section, core, head = lax.axis_index("section"), lax.axis_index("core"), lax.axis_index("head")
     y, z = lax.axis_index("y"), lax.axis_index("z")
     peers = {
@@ -297,7 +388,7 @@
         "y+": {"y": (y + 1) % NY}, "y-": {"y": (y + NY - 1) % NY},
         "z+": {"z": (z + 1) % NZ}, "z-": {"z": (z + NZ - 1) % NZ},
     }
-    count = [0]
+    count = [0, 0]
     sends = []
 
     def send(src, dst, to):
@@ -316,95 +407,108 @@
             copy.wait_send()
             sends[:] = [c for c in sends if c is not copy]
 
-    loads = [
-        pltpu.make_async_copy(src, dst, local_sem.at[at])
-        for at, (src, dst) in enumerate((
-            (blocks.at[:, 1], vals_in), (kv_own, kv.at[(core * NY + y) * NZ + z]), (blocks.at[:, 0], keys_in), (weight, w),
-        ))
-    ]
-    for load in loads:
-        load.start()
+    def local(src, dst):
+        copy = pltpu.make_async_copy(src, dst, local_sem.at[count[1]])
+        count[1] += 1
+        copy.start()
+        return copy
+
+    part_rows = blocks.shape[2] // PARTS
+    slot = part_rows * blocks.shape[3] * 2e-6
+
+    def rows_of(ref, kind, part):
+        return ref.at[:, kind, pl.ds(part * part_rows, part_rows)]
+
+    def shard_at(c, yy, zz):
+        return (c * NY + yy) * NZ + zz
+
+    own = kv.at[shard_at(core, y, z)]
+    parts = [buffers[p * 12 : (p + 1) * 12] for p in range(PARTS)]
+    load_kv = local(kv_own, own)
+    load_vals = [local(rows_of(blocks, 1, p), parts[p][1]) for p in range(PARTS)]
+    load_keys = [local(rows_of(blocks, 0, p), parts[p][0]) for p in range(PARTS)]
+    load_weight = local(weight, w)
     barrier = pltpu.get_barrier_semaphore()
     for peer in peers.values():
         pl.semaphore_signal(barrier, inc=1, device_id=peer, device_id_type=pl.DeviceIdType.MESH)
     pl.semaphore_wait(barrier, len(peers))
 
-    def first_hops(stage, arrivals, axis, caps):
+    def around(stage, arrivals, axis, caps, column, pools):
         cap, back = caps[0], sum(caps)
-        return [
-            send(stage.at[pl.ds(0, cap)], arrivals.at[pl.ds(0, cap)], axis + "+"),
-            send(stage.at[pl.ds(cap, cap)], arrivals.at[pl.ds(back, cap)], axis + "-"),
-        ]
-
-    def next_hops(before, arrivals, axis, caps, k):
-        came, at, back = sum(caps[: k - 1]), sum(caps[:k]), sum(caps)
-        hops = []
-        for copy, base, to in ((before[0], 0, "+"), (before[1], back, "-")):
-            copy.wait_recv()
-            hops.append(send(
-                arrivals.at[pl.ds(base + came, caps[k])], arrivals.at[pl.ds(base + at, caps[k])], axis + to
-            ))
-        return hops
-
-    def arrived(hops):
-        for copy in hops:
-            copy.wait_recv()
-
-    def pick_lists(stage, caps, column, pools):
-        pick(stage.at[pl.ds(0, caps[0])], caps[0], picks, column, pools)
-        pick(stage.at[pl.ds(caps[0], caps[0])], caps[0], picks, column + 1, pools)
-
-    def shard_at(c, yy, zz):
-        return (c * NY + yy) * NZ + zz
-
-    loads[1].wait()
-    own = kv.at[shard_at(core, y, z)]
-    kv_hops = [send(own, own, "z+"), send(own, own, "z-")]
-    loads[0].wait()
-    swap_vals = send(vals_in, vals_0, "x")
-    loads[2].wait()
-    pick_lists(keys_st, Z_FIRST, KEYS_COL, [keys_in])
-    keys_from = keys_z = first_hops(keys_st, keys_1, "z", Z_FIRST)
-
-    for k in range(1, NZ // 2):
-        kv_hops[0].wait_recv()
-        kv_hops[1].wait_recv()
-        ahead = kv.at[shard_at(core, y, (z - k + NZ) % NZ)]
-        back = kv.at[shard_at(core, y, (z + k) % NZ)]
-        kv_hops[0] = send(ahead, ahead, "z+")
-        if k < NZ // 2 - 1:
-            kv_hops[1] = send(back, back, "z-")
-    kv_hops[0].wait_recv()
-
-    def line(yy):
-        return kv.at[pl.ds(shard_at(core, yy, 0), NZ)]
-
-    def part(yy, first):
-        return kv.at[pl.ds(shard_at(core, yy, first), NZ // 2)]
-
-    over, under = (y + 1) % NY, (y + NY - 1) % NY
-    kv_y = [send(line(y), line(y), "y+"), send(line(y), line(y), "y-")]
-    kv_core = [send(line(y), line(y), "core")]
-    high[...] = jnp.full_like(high, -1e30)
-    total[...] = jnp.zeros_like(total)
-    accum[...] = jnp.zeros_like(accum)
-    keys_z = next_hops(keys_z, keys_1, "z", Z_FIRST, 1)
-    kv_y[0].wait_recv()
-    kv_far = [send(part(under, 0), part(under, 0), "y+")]
-    kv_core.append(send(line(under), line(under), "core"))
-    kv_y[1].wait_recv()
-    kv_far.append(send(part(over, NZ // 2), part(over, NZ // 2), "y-"))
-    kv_core.append(send(line(over), line(over), "core"))
-    swap_vals.wait_recv()
-    pick_lists(vals_st, Y_FIRST, VALS_COL, [vals_0])
-    vals_from = vals_y = first_hops(vals_st, vals_1, "y", Y_FIRST)
-    keys_z = next_hops(keys_z, keys_1, "z", Z_FIRST, 2)
-    arrived(kv_far)
-    kv_core.append(send(line((y + 2) % NY), line((y + 2) % NY), "core"))
-    arrived(kv_core)
+        ways = ((0, axis + "+", 0), (1, axis + "-", back))
+        for at, to, base in ways:
+            pick(stage, at * cap, cap, picks, column + at, pools)
+        from_stage = Transfer(axis, cap * slot, *[
+            (stage.at[pl.ds(at * cap, cap)], arrivals.at[pl.ds(base, cap)], to) for at, to, base in ways
+        ])
+        yield from_stage
+        for k in range(1, len(caps)):
+            came, at = sum(caps[: k - 1]), sum(caps[:k])
+            yield Transfer(axis, caps[k] * slot, *[
+                (arrivals.at[pl.ds(base + came, caps[k])], arrivals.at[pl.ds(base + at, caps[k])], to)
+                for _, to, base in ways
+            ])
+        sent(from_stage.copies)
+
+    def between_cores(stage, arrivals, column, pools):
+        pick(stage, 0, BLK_DEV, picks, column, pools)
+        crossing = Transfer("core", BLK_DEV * slot, (stage.at[pl.ds(0, BLK_DEV)], arrivals, "core"))
+        yield crossing
+        sent(crossing.copies)
+
+    outs = []
+
+    def keys_chain(part):
+        held, _, _, stage, came_1, came_2, came_3, last = parts[part][:8]
+        load_keys[part].wait()
+        yield from around(stage, came_1, "z", Z_FIRST, KEYS_COL, [held])
+        yield from around(stage, came_2, "y", Y_SECOND, KEYS_COL + 2, [held, came_1])
+        yield from between_cores(stage, came_3, KEYS_COL + 4, [held, came_1, came_2])
+        pick(stage, 0, BLK_DEV, picks, KEYS_COL + 5, [held, came_1, came_2, came_3])
+        yield Transfer("x", BLK_DEV * slot, (stage.at[pl.ds(0, BLK_DEV)], last, "x"))
+        outs.append(local(last, rows_of(decoded, 0, part)))
+
+    def vals_chain(part):
+        _, inside, held = parts[part][:3]
+        stage, came_1, came_2, came_3 = parts[part][8:]
+        load_vals[part].wait()
+        swap = Transfer("x", BLK_DEV * slot, (inside, held, "x"))
+        yield swap
+        yield from around(stage, came_1, "y", Y_FIRST, VALS_COL, [held])
+        yield from around(stage, came_2, "z", Z_SECOND, VALS_COL + 2, [held, came_1])
+        yield from between_cores(stage, came_3, VALS_COL + 4, [held, came_1, came_2])
+        sent(swap.copies)
+        pick(inside, 0, BLK_DEV, picks, VALS_COL + 5, [held, came_1, came_2, came_3])
+        outs.append(local(inside, rows_of(decoded, 1, part)))
 
     first_query = ((y * NZ + z) * NC + core) * TOK_ROWS
     local_kv, rows, _ = spread.shape
+    group = rows // TOK_ROWS
+
+    def row_limits():
+        tile_of = requests[pl.ds((y * NZ + z) * NC + core, 1), :]
+        starts = jnp.zeros(tile_of.shape, jnp.float32)
+        for r in range(1, REQUESTS):
+            earlier = jnp.where(requests[...] < r, 1.0, 0.0)
+            first = jnp.sum(jnp.sum(earlier, axis=1, keepdims=True), axis=0, keepdims=True)
+            starts = jnp.where(tile_of == r, first, starts)
+        places = (lax.broadcasted_iota(jnp.int32, tile_of.shape, 1) + first_query).astype(jnp.float32)
+        return jnp.concatenate([starts] * group, axis=1), jnp.concatenate([places] * group, axis=1)
+
+    def prepare():
+        high[...] = jnp.full_like(high, -1e30)
+        total[...] = jnp.zeros_like(total)
+        accum[...] = jnp.zeros_like(accum)
+        spread[...] = jnp.zeros_like(spread)
+        for c in range(local_kv):
+            for g in range(group):
+                at = (c * group + g) * HD
+                spread[c, g * TOK_ROWS : (g + 1) * TOK_ROWS, c * HD : (c + 1) * HD] = queries[
+                    :, at : at + HD
+                ] * jnp.bfloat16(1.0 / math.sqrt(HD))
+        starts, places = row_limits()
+        high[4:5, :] = starts
+        high[5:6, :] = places
 
     def slab(half):
         unit, of_core = half // NC, half % NC
@@ -413,7 +517,8 @@
         keys, vals = block[:, : local_kv * HD], block[:, local_kv * HD :].T
         row = lax.broadcasted_iota(jnp.int32, (SLAB, rows), 0)
         pos = unit * UNIT + of_core * TOK_ROWS + (row // TOK_ROWS) * (NC * TOK_ROWS) + row % TOK_ROWS
-        keep = (pos >= limits[0:1, :]) & (pos <= limits[1:2, :])
+        pos = pos.astype(jnp.float32)
+        keep = (pos >= high[4:5, :]) & (pos <= high[5:6, :])
         for c in range(local_kv):
             scores = lax.dot_general(
                 keys, spread[c], (((1,), (1,)), ((), ())), preferred_element_type=jnp.float32
@@ -441,79 +546,87 @@
 
         lax.fori_loop(low * NC, top * NC, one, 0)
 
-    units(0, 2)
-    keys_z = next_hops(keys_z, keys_1, "z", Z_FIRST, 3)
-    vals_y = next_hops(vals_y, vals_1, "y", Y_FIRST, 1)
-    arrived(keys_z)
-    sent(keys_from)
-    pick_lists(keys_st, Y_SECOND, KEYS_COL + 2, [keys_in, keys_1])
-    keys_from = keys_y = first_hops(keys_st, keys_2, "y", Y_SECOND)
-    arrived(vals_y)
-    sent(vals_from)
-    pick_lists(vals_st, Z_SECOND, VALS_COL + 2, [vals_0, vals_1])
-    vals_from = vals_z = first_hops(vals_st, vals_2, "z", Z_SECOND)
-    units(2, 6)
-    keys_y = next_hops(keys_y, keys_2, "y", Y_SECOND, 1)
-    vals_z = next_hops(vals_z, vals_2, "z", Z_SECOND, 1)
-    arrived(keys_y)
-    sent(keys_from)
-
-    def between_cores(stage, arrivals, column, pools):
-        pick(stage.at[pl.ds(0, BLK_DEV)], BLK_DEV, picks, column, pools)
-        return send(stage.at[pl.ds(0, BLK_DEV)], arrivals, "core")
-
-    keys_pools = [keys_in, keys_1, keys_2, keys_3]
-    vals_pools = [vals_0, vals_1, vals_2, vals_3]
-    crossing = between_cores(keys_st, keys_3, KEYS_COL + 4, keys_pools[:3])
-    crossing.wait_recv()
-    sent([crossing])
-    pick(keys_st.at[pl.ds(0, BLK_DEV)], BLK_DEV, picks, KEYS_COL + 5, keys_pools)
-    swap_keys = send(keys_st.at[pl.ds(0, BLK_DEV)], keys_end, "x")
-    units(6, 8)
-    vals_z = next_hops(vals_z, vals_2, "z", Z_SECOND, 2)
-
-    group = rows // TOK_ROWS
-    for c in range(local_kv):
-        done = (accum[c] / total[c : c + 1, :]).astype(jnp.bfloat16)
-        for g in range(group):
-            at = (c * group + g) * HD
-            att[at : at + HD, :] = done[:, g * TOK_ROWS : (g + 1) * TOK_ROWS]
-    loads[3].wait()
-    width = w.shape[1] // 2
-    attended = att[...].T
-
-    def columns(first):
-        return jnp.dot(attended, w[:, pl.ds(pl.multiple_of(first, width), width)], preferred_element_type=jnp.float32)
-
-    away[...] = columns((1 - head) * width).astype(jnp.bfloat16)
-    over_heads = send(away, got, "head")
-    kept_out[...] = columns(head * width)
-    vals_z = next_hops(vals_z, vals_2, "z", Z_SECOND, 3)
-    over_heads.wait_recv()
-    mixed[...] = (kept_out[...] + got[...].astype(jnp.float32)).astype(jnp.bfloat16)
-
-    arrived(vals_z)
-    sent(vals_from)
-    crossing = between_cores(vals_st, vals_3, VALS_COL + 4, vals_pools[:3])
-    crossing.wait_recv()
-    sent([crossing])
-    sent([swap_vals])
-    pick(vals_in, BLK_DEV, picks, VALS_COL + 5, vals_pools)
-    vals_out = pltpu.make_async_copy(vals_in, decoded.at[:, 1], local_sem.at[4])
-    vals_out.start()
-    swap_keys.wait_recv()
-    keys_out = pltpu.make_async_copy(keys_end, decoded.at[:, 0], local_sem.at[5])
-    keys_out.start()
-    vals_out.wait()
-    keys_out.wait()
+    def tokens_chain():
+        shard = kv_own.shape[0] * kv_own.shape[1] * 2e-6
+        load_kv.wait()
+        yield Transfer("z", shard, (own, own, "z+"), (own, own, "z-"), small=True)
+        for k in range(1, NZ // 2):
+            ahead = kv.at[shard_at(core, y, (z - k + NZ) % NZ)]
+            back = kv.at[shard_at(core, y, (z + k) % NZ)]
+            moves = [(ahead, ahead, "z+")]
+            if k < NZ // 2 - 1:
+                moves.append((back, back, "z-"))
+            yield Transfer("z", shard, *moves, small=True)
+
+        def line(yy):
+            return kv.at[pl.ds(shard_at(core, yy, 0), NZ)]
+
+        def some(yy, first):
+            return kv.at[pl.ds(shard_at(core, yy, first), NZ // 2)]
+
+        def to_core(yy):
+            crossing = Transfer("core", NZ * shard, (line(yy), line(yy), "core"))
+            order.post(crossing, 0)
+            return crossing
+
+        over, under, across = (y + 1) % NY, (y + NY - 1) % NY, (y + 2) % NY
+        around_y = Transfer("y", NZ * shard, (line(y), line(y), "y+"), (line(y), line(y), "y-"))
+        order.post(around_y, FIRST_Y["tokens"])
+        crossings = [to_core(y)]
+        prepare()
+        yield around_y
+        far = Transfer(
+            "y", NZ // 2 * shard,
+            (some(under, 0), some(under, 0), "y+"), (some(over, NZ // 2), some(over, NZ // 2), "y-"),
+        )
+        order.post(far, FIRST_Y["far"])
+        crossings += [to_core(under), to_core(over)]
+        yield far
+        crossings.append(to_core(across))
+        for crossing in crossings:
+            yield crossing
+        for unit in range(kv.shape[0] * TOK_ROWS // UNIT):
+            yield None
+            units(unit, unit + 1)
+
+        for c in range(local_kv):
+            done = (accum[c] / total[c : c + 1, :]).astype(jnp.bfloat16)
+            for g in range(group):
+                at = (c * group + g) * HD
+                att[at : at + HD, :] = done[:, g * TOK_ROWS : (g + 1) * TOK_ROWS]
+        load_weight.wait()
+        width = w.shape[1] // 2
+        attended = att[...].T
+
+        def columns(first):
+            first = pl.multiple_of(first, width)
+            return jnp.dot(attended, w[:, pl.ds(first, width)], preferred_element_type=jnp.float32)
+
+        away[...] = columns((1 - head) * width).astype(jnp.bfloat16)
+        over_heads = Transfer("head", 0.26, (away, got, "head"))
+        order.post(over_heads, 0)
+        kept_out[...] = columns(head * width)
+        yield over_heads
+        mixed[...] = (kept_out[...] + got[...].astype(jnp.float32)).astype(jnp.bfloat16)
+
+    order = Order(send)
+    chains = [("tokens", tokens_chain())]
+    chains += [("vals%d" % part, vals_chain(part)) for part in range(PARTS)]
+    chains += [("keys%d" % part, keys_chain(part)) for part in range(PARTS)]
+    order.run(chains)
+    for copy in outs:
+        copy.wait()
     sent(sends[:])
 
 
-def move_and_multiply(picks, spread, kv_own, limits, weight, blocks):
-    local_kv, rows, _ = spread.shape
-    half = lambda n: pltpu.VMEM((n,) + blocks.shape[2:], blocks.dtype)
+def move_and_multiply(picks, queries, kv_own, requests, weight, blocks):
+    local_kv = kv_own.shape[1] // (2 * HD)
+    rows = HEADS // KVH * TOK_ROWS
+    part_rows = blocks.shape[2] // PARTS
+    half = lambda n: pltpu.VMEM((n, part_rows) + blocks.shape[3:], blocks.dtype)
     vmem, hbm = pl.BlockSpec(memory_space=pltpu.VMEM), pl.BlockSpec(memory_space=pl.ANY)
     width = weight.shape[1] // 2
+    copies = 16 + PARTS * 28
     return pl.pallas_call(
         move_kernel,
         out_shape=(
@@ -525,9 +638,7 @@
         scratch_shapes=[
             pltpu.VMEM((SHARDS,) + kv_own.shape, jnp.bfloat16),
             pltpu.VMEM(weight.shape, jnp.bfloat16),
-            half(BLK_DEV), half(BLK_DEV), half(BLK_DEV),
-            half(2 * max(Z_FIRST[0], Y_SECOND[0])), half(2 * sum(Z_FIRST)), half(2 * sum(Y_SECOND)), half(BLK_DEV), half(BLK_DEV),
-            half(2 * max(Y_FIRST[0], Z_SECOND[0])), half(2 * sum(Y_FIRST)), half(2 * sum(Z_SECOND)), half(BLK_DEV),
+            pltpu.VMEM((local_kv, rows, local_kv * HD), jnp.bfloat16),
             pltpu.VMEM((8, rows), jnp.float32),
             pltpu.VMEM((8, rows), jnp.float32),
             pltpu.VMEM((local_kv, HD, rows), jnp.float32),
@@ -535,35 +646,31 @@
             pltpu.VMEM((TOK_ROWS, width), jnp.float32),
             pltpu.VMEM((TOK_ROWS, width), jnp.bfloat16),
             pltpu.VMEM((TOK_ROWS, width), jnp.bfloat16),
-            pltpu.SemaphoreType.DMA((6,)),
-            pltpu.SemaphoreType.DMA((N_COPIES,)),
-            pltpu.SemaphoreType.DMA((N_COPIES,)),
+            pltpu.SemaphoreType.DMA((2 + 4 * PARTS,)),
+            pltpu.SemaphoreType.DMA((copies,)),
+            pltpu.SemaphoreType.DMA((copies,)),
+        ]
+        + [
+            half(n)
+            for _ in range(PARTS)
+            for n in (
+                BLK_DEV, BLK_DEV, BLK_DEV,
+                2 * max(Z_FIRST[0], Y_SECOND[0]), 2 * sum(Z_FIRST), 2 * sum(Y_SECOND), BLK_DEV, BLK_DEV,
+                2 * max(Y_FIRST[0], Z_SECOND[0]), 2 * sum(Y_FIRST), 2 * sum(Z_SECOND), BLK_DEV,
+            )
         ],
         compiler_params=pltpu.CompilerParams(
             collective_id=0, has_side_effects=True, vmem_limit_bytes=63 * 1024 * 1024
         ),
         cost_estimate=pl.CostEstimate(flops=10**10, bytes_accessed=20 * 2**20, transcendentals=10**7),
-    )(picks, spread, kv_own, limits, weight, blocks)
+    )(picks, queries, kv_own, requests, weight, blocks)
 
 
 def per_device(queries, keyvals, span_req, prefill_blocks, block_dest, out_weight):
-    tok_rows = queries.shape[1]
-    local_kv = keyvals.shape[3] // HD
-    group = HEADS // KVH
-    tok = (lax.axis_index("y") * NZ + lax.axis_index("z")) * NC + lax.axis_index("core")
-    first_query = tok * tok_rows
-    segments = span_req[0]
-
     picks, room = plan(block_dest)
-    own_segments = lax.dynamic_slice_in_dim(segments, first_query, tok_rows)
-    starts = jnp.sum(segments[None, :] < own_segments[:, None], axis=1).astype(jnp.int32)
-    places = first_query + jnp.arange(tok_rows, dtype=jnp.int32)
-    limits = jnp.stack([jnp.tile(starts, group), jnp.tile(places, group)])
-    scaled = queries[0].reshape(tok_rows, local_kv, group, HD) * jnp.bfloat16(1.0 / math.sqrt(HD))
-    own = jnp.eye(local_kv, dtype=jnp.bfloat16)
-    spread = jnp.einsum("qcgd,ce->cgqed", scaled, own).reshape(local_kv, group * tok_rows, local_kv * HD)
-    kv_own = keyvals[0].reshape(tok_rows, 2 * local_kv * HD)
-    mixed, routed = move_and_multiply(picks, spread, kv_own, limits, out_weight, prefill_blocks)
+    kv_own = keyvals[0].reshape(TOK_ROWS, -1)
+    requests = span_req.reshape(SHARDS, TOK_ROWS)
+    mixed, routed = move_and_multiply(picks, queries[0], kv_own, requests, out_weight, prefill_blocks)
     decode_blocks = lax.cond(
         room[0, 0] <= 0.0,
         lambda done, blocks, dest: done,

time: 228 us -> 192 us (0.84)
  Pallas kernels: 210 us -> 180 us
  local copies, waits for them, and re-layouts: 13.4 us -> 9.93 us
  other arithmetic: 3.14 us -> 0.72 us
    pallas_call x1, Pallas kernels: 207 us -> 177 us  [move_and_multiply(): pl.pallas_call(move_kernel, out_shape=(jax.ShapeDtypeStruct((TOK_ROWS, wi...]
    unnamed x8 -> x7, local copies, waits for them, and re-layouts: 8 us -> 7.11 us
where the time goes in v2:
time: 192 us
  Pallas kernels  180 us (94%)
  local copies, waits for them, and re-layouts  9.93 us (5%)
    pallas_call x1, Pallas kernels, move_and_multiply(): pl.pallas_call(move_kernel, out_shape=(jax.ShapeDtypeStruct((TOK_ROWS, wi...  177 us
    unnamed x7, local copies, waits for them, and re-layouts  7.11 us

profile of v2, /device:TPU:1, one launch (start us, length us, event | category | flops | bytes accessed | tf_op | source)
XLA Modules:
  0.0 191.8 jit_solution(15316830218238344560)
XLA Ops:
  0.6 0.7 add_select_fusion
  1.4 0.1 reshape.92
  1.6 0.7 reshape.94.by_z
  2.3 0.1 reshape.93
  2.4 0.6 pad.9.by_y
  3.0 2.3 %shard_map.77 = (s32[32,128]{1,0:T(8,128)}, f32[8,128]{1,0:T(8,128)}) custom-call(s32[2,2,8,256]{3,2,1,0:T(8,128)} %pad.9.by_y, s32[2,2,8,128]{3,2,1,0:T(8,128)} %reshape.94.by_z), custom_call_target="tpu_custom_call" | custom-call | tf_op jit(solution)/shard_map/pallas_call | solution.py:258
  5.3 1.2 slice.3
  7.2 1.6 copy.16
  8.7 0.0 copy-start.1
  8.7 177.5 %shard_map.78 = (bf16[128,1024]{1,0:T(8,128)(2,1)}, bf16[24,2,128,256]{3,2,1,0:T(8,128)(2,1)}) custom-call(s32[32,128]{1,0:T(8,128)} %get-tuple-element.18.picks, bf16[128,1024]{1,0:T(8,128)(2,1)} %bitcast.20, bf16[128,512]{1,0:T(8,128)(2,1)} %bitcast.19, s32[64,128]{1,0:T(8,128)} %bitcast.21, bf16[1024,2048]{1,0:T(8,128)(2,1)} %weight.1, ...), custom_call_target="tpu_custom_call" | custom-call | flops 10000000000 | bytes 20971520 | tf_op jit(solution)/shard_map/pallas_call | solution.py:630
  186.2 0.0 copy-done.1
  186.3 0.0 copy-start
  186.3 0.9 copy-done
  187.2 0.7 copy.21
  187.9 3.9 %copy.22 = bf16[24,2,128,256]{3,2,1,0:T(8,128)(2,1)} copy(bf16[24,2,128,256]{3,2,1,0:T(8,128)(2,1)} %get-tuple-element.28) | data formatting | bytes 6291456
  (4 shorter events, 0.1 us)
Async XLA Ops:
  8.7 177.5 %copy-start.1 = (s32[3072]{0:T(1024)S(1)}, s32[3072]{0:T(1024)}, u32[]{:S(2)}) copy-start(s32[3072]{0:T(1024)} %param.12) | copy-start | bytes 36868
  186.3 1.0 copy-start

commit v3 on v2

--- a/solution.py
+++ b/solution.py
@@ -239,7 +239,7 @@
         for c in range(NC):
             worst = jnp.maximum(worst, list_room(by_y[half, c], False))
             worst = jnp.maximum(worst, list_room(by_z[half, c], True))
-    room[...] = jnp.full(room.shape, worst, jnp.float32)
+    room[0, 0] = worst
 
 
 def plan_tables(block_dest):
@@ -257,9 +257,9 @@
     vmem = pl.BlockSpec(memory_space=pltpu.VMEM)
     return pl.pallas_call(
         plan_kernel,
-        out_shape=(jax.ShapeDtypeStruct((32, 128), jnp.int32), jax.ShapeDtypeStruct((8, 128), jnp.float32)),
+        out_shape=(jax.ShapeDtypeStruct((32, 128), jnp.int32), jax.ShapeDtypeStruct((1, 1), jnp.float32)),
         in_specs=[vmem, vmem],
-        out_specs=(vmem, vmem),
+        out_specs=(vmem, pl.BlockSpec(memory_space=pltpu.SMEM)),
     )(*plan_tables(block_dest))
 
 
@@ -607,7 +607,8 @@
         order.post(over_heads, 0)
         kept_out[...] = columns(head * width)
         yield over_heads
-        mixed[...] = (kept_out[...] + got[...].astype(jnp.float32)).astype(jnp.bfloat16)
+        got[...] = (kept_out[...] + got[...].astype(jnp.float32)).astype(jnp.bfloat16)
+        outs.append(local(got, mixed))
 
     order = Order(send)
     chains = [("tokens", tokens_chain())]
@@ -634,7 +635,7 @@
             jax.ShapeDtypeStruct(blocks.shape, blocks.dtype),
         ),
         in_specs=[pl.BlockSpec(memory_space=pltpu.SMEM), vmem, hbm, vmem, hbm, hbm],
-        out_specs=(vmem, hbm),
+        out_specs=(hbm, hbm),
         scratch_shapes=[
             pltpu.VMEM((SHARDS,) + kv_own.shape, jnp.bfloat16),
             pltpu.VMEM(weight.shape, jnp.bfloat16),
@@ -646,7 +647,7 @@
             pltpu.VMEM((TOK_ROWS, width), jnp.float32),
             pltpu.VMEM((TOK_ROWS, width), jnp.bfloat16),
             pltpu.VMEM((TOK_ROWS, width), jnp.bfloat16),
-            pltpu.SemaphoreType.DMA((2 + 4 * PARTS,)),
+            pltpu.SemaphoreType.DMA((3 + 4 * PARTS,)),
             pltpu.SemaphoreType.DMA((copies,)),
             pltpu.SemaphoreType.DMA((copies,)),
         ]

time: 192 us -> 190 us (0.990)
  no operation moved by 1% of the time
where the time goes in v3:
time: 190 us
  Pallas kernels  179 us (94%)
  local copies, waits for them, and re-layouts  8.75 us (5%)
    pallas_call x1, Pallas kernels, move_and_multiply(): pl.pallas_call(move_kernel, out_shape=(jax.ShapeDtypeStruct((TOK_ROWS, wi...  177 us
    unnamed x7, local copies, waits for them, and re-layouts  7.11 us

profile of v3, /device:TPU:1, one launch (start us, length us, event | category | flops | bytes accessed | tf_op | source)
XLA Modules:
  0.0 189.7 jit_solution(8506590185025909091)
XLA Ops:
  0.6 0.7 add_select_fusion
  1.4 0.1 reshape.92
  1.6 0.7 reshape.94.by_z
  2.3 0.1 reshape.93
  2.4 0.6 pad.9.by_y
  3.0 2.2 %shard_map.77 = (s32[32,128]{1,0:T(8,128)}, f32[1,1]{1,0:T(1,128)}) custom-call(s32[2,2,8,256]{3,2,1,0:T(8,128)} %pad.9.by_y, s32[2,2,8,128]{3,2,1,0:T(8,128)} %reshape.94.by_z), custom_call_target="tpu_custom_call" | custom-call | tf_op jit(solution)/shard_map/pallas_call | solution.py:258
  5.8 1.6 copy.16
  7.4 0.0 copy-start.1
  7.4 176.7 %shard_map.78 = (bf16[128,1024]{1,0:T(8,128)(2,1)}, bf16[24,2,128,256]{3,2,1,0:T(8,128)(2,1)}) custom-call(s32[32,128]{1,0:T(8,128)} %get-tuple-element.18.picks, bf16[128,1024]{1,0:T(8,128)(2,1)} %bitcast.20, bf16[128,512]{1,0:T(8,128)(2,1)} %bitcast.19, s32[64,128]{1,0:T(8,128)} %bitcast.21, bf16[1024,2048]{1,0:T(8,128)(2,1)} %weight.1, ...), custom_call_target="tpu_custom_call" | custom-call | flops 10000000000 | bytes 20971520 | tf_op jit(solution)/shard_map/pallas_call | solution.py:631
  184.2 0.0 copy-done.1
  184.2 0.0 copy-start
  184.2 0.9 copy-done
  185.1 0.7 copy.21
  185.8 3.9 %copy.22 = bf16[24,2,128,256]{3,2,1,0:T(8,128)(2,1)} copy(bf16[24,2,128,256]{3,2,1,0:T(8,128)(2,1)} %get-tuple-element.28) | data formatting | bytes 6291456
  (4 shorter events, 0.1 us)
Async XLA Ops:
  7.4 176.8 %copy-start.1 = (s32[3072]{0:T(1024)S(1)}, s32[3072]{0:T(1024)}, u32[]{:S(2)}) copy-start(s32[3072]{0:T(1024)} %param.12) | copy-start | bytes 36868
  184.2 1.0 copy-start
